TPU v7x, 32 devices: a whole 2x2x4 slice. The times are simulated.
32 devices in a mesh: row: 2 (over x), col: 16 (over z, y, core).
Axes of the slice: x: 2, y: 2, z: 4, core: 2. Of those that a mesh axis runs over, the one named last changes fastest.
Arguments:
- sigma_anc: bfloat16 [4096, 4096], P('row', 'col'), as said below
- top_panel: bfloat16 [4096, 4096], P('row', 'col'), may hold values from -0.09375 to 0.09375
- top_dinv: bfloat16 [4096, 4096], P('row', 'col'), as said below
- low_upper: bfloat16 [4096, 4096], P('row', 'col'), may hold values from -0.09375 to 0.09375
- low_ancestor: bfloat16 [4096, 4096], P('row', 'col'), may hold values from -0.09375 to 0.09375
- low_dinv: bfloat16 [4096, 4096], P('row', 'col'), as said below
- low_rows: int32 [16], replicated, may hold values from 0 to 31, as said below
Outputs:
- top_off: bfloat16 [4096, 4096], P('row', 'col')
- top_diag: bfloat16 [4096, 4096], P('row', 'col')
- low_top: bfloat16 [4096, 4096], P('row', 'col')
- low_anc: bfloat16 [4096, 4096], P('row', 'col')
- low_diag: bfloat16 [4096, 4096], P('row', 'col')
Inputs may be any that keep to these rules, and one draw needn't show every extreme that they name: `low_rows`: 16 distinct block indices; the first and the last ancestor block are always among them. `sigma_anc`: symmetric. `top_dinv`: symmetric. `low_dinv`: symmetric.
All inputs are finite; a program needn't handle non-finite values.
Results may differ from a plain program's by a relative error of at most 0.0085.
Values may be sent and summed in bfloat16 or wider, within the bound.
No kernel may reach another device: no remote copies, remote signals or barrier semaphores. Data moves between devices by JAX's collectives and lax.ppermute only.
A program may use at most 128 MiB of HBM per device.

v0:
```python
import jax
import jax.numpy as jnp
from jax import lax
from jax.sharding import PartitionSpec as P

BLOCK = 128


def times_rows(columns, block_part):
    return jnp.dot(block_part, columns, preferred_element_type=jnp.float32)


def inner_rows(left, right):
    return lax.dot_general(
        left, right, (((0,), (0,)), ((), ())), preferred_element_type=jnp.float32
    )


def body(sigma_anc, top_panel, top_dinv, low_upper, low_ancestor, low_dinv, low_rows):
    rows_here = sigma_anc.shape[0]
    width_here = top_panel.shape[1]
    row_ids = (lax.axis_index("row") * rows_here + jnp.arange(rows_here, dtype=jnp.int32)) // BLOCK
    in_pattern = jnp.any(row_ids[:, None] == low_rows[None, :], axis=1).astype(jnp.float32)[:, None]
    masked = (low_ancestor.astype(jnp.float32) * in_pattern).astype(jnp.bfloat16)
    top_cols, masked_cols, upper_cols = (
        lax.all_gather(top_panel, "row", axis=0, tiled=True),
        lax.all_gather(masked, "row", axis=0, tiled=True),
        lax.all_gather(low_upper, "row", axis=0, tiled=True),
    )
    top_product = times_rows(top_cols, lax.all_gather(sigma_anc, "col", axis=1, tiled=True))
    top_off = (-top_product).astype(jnp.bfloat16)
    block_part = lax.all_gather(top_off, "col", axis=1, tiled=True)
    terms = jnp.concatenate(
        [inner_rows(block_part, top_panel), inner_rows(block_part, masked)], axis=1
    )
    carried = times_rows(upper_cols, lax.all_gather(top_off, "col", axis=1, tiled=True))
    diag_total = lax.psum_scatter(terms[:, :width_here], "row", scatter_dimension=0, tiled=True)
    top_diag = (top_dinv.astype(jnp.float32) - diag_total).astype(jnp.bfloat16)
    upper_part = times_rows(upper_cols, lax.all_gather(top_diag, "col", axis=1, tiled=True))
    cross_total = lax.psum_scatter(
        terms[:, width_here:].astype(jnp.bfloat16), "row", scatter_dimension=0, tiled=True
    ).astype(jnp.float32)
    low_top = (-(upper_part + cross_total)).astype(jnp.bfloat16)
    low_product = times_rows(masked_cols, lax.all_gather(sigma_anc, "col", axis=1, tiled=True))
    low_anc = (-in_pattern * (carried + low_product)).astype(jnp.bfloat16)
    upper_count = low_top.shape[0]
    stacked = jnp.concatenate([low_top, low_anc], axis=0)
    block_part = lax.all_gather(stacked, "col", axis=1, tiled=True)
    low_terms = inner_rows(block_part[:upper_count], low_upper) + inner_rows(
        block_part[upper_count:], masked
    )
    low_sum = lax.psum_scatter(low_terms, "row", scatter_dimension=0, tiled=True)
    low_diag = (low_dinv.astype(jnp.float32) - low_sum).astype(jnp.bfloat16)
    return (top_off, top_diag, low_top, low_anc, low_diag)


def solution(mesh):
    in_specs = (
        P("row", "col"),
        P("row", "col"),
        P("row", "col"),
        P("row", "col"),
        P("row", "col"),
        P("row", "col"),
        P(),
    )
    out_specs = (
        P("row", "col"),
        P("row", "col"),
        P("row", "col"),
        P("row", "col"),
        P("row", "col"),
    )
    return jax.shard_map(body, mesh=mesh, in_specs=in_specs, out_specs=out_specs, check_vma=False)
```

profile of v0, /device:TPU:0, one launch (start us, length us, event | category | flops | bytes accessed | tf_op | source)
XLA Modules:
  0.0 889.5 jit_solution(7573896253649476623)
XLA Ops:
  7.2 0.7 all-gather.10.cloned.1.call-update
  7.9 0.7 all-gather.8.cloned.1.call-update
  8.7 36.7 %all-gather.10.cloned.1.call-done = bf16[4096,256]{1,0:T(8,128)(2,1)} async-done(((bf16[2048,256]{1,0:T(8,128)(2,1)}), bf16[4096,256]{1,0:T(8,128)(2,1)}) %all-gather.10.cloned.1.call-update) | async-done | bytes 2097168 | tf_op jit(solution)/shard_map/all_gather | solution.py:26
  45.4 132.5 %all-gather.8.cloned.1.call-done = bf16[2048,4096]{1,0:T(8,128)(2,1)} async-done(((bf16[2048,256]{1,0:T(8,128)(2,1)}), bf16[2048,4096]{1,0:T(8,128)(2,1)}) %all-gather.8.cloned.1.call-update) | async-done | bytes 16777232 | tf_op jit(solution)/shard_map/all_gather | solution.py:30
  177.9 12.0 %fusion.7 = bf16[2048,256]{1,0:T(8,128)(2,1)} fusion(bf16[2048,4096]{1,0:T(8,128)(2,1)} %all-gather.8.cloned.1.call-done, bf16[4096,256]{1,0:T(8,128)(2,1)} %all-gather.10.cloned.1.call-done), kind=kOutput, calls=%fused_computation.8 | convolution fusion | flops 4296015872 | bytes 19922944 | tf_op jit(solution)/shard_map/dot_general | solution.py:10
  190.0 0.0 reduce-scatter.4.cloned.1.call-start
  190.0 128.6 %all-gather.12.cloned.1.call-done = bf16[2048,4096]{1,0:T(8,128)(2,1)} async-done(((bf16[2048,256]{1,0:T(8,128)(2,1)}), bf16[2048,4096]{1,0:T(8,128)(2,1)}) %all-gather.12.cloned.1.call-update) | async-done | bytes 16777232 | tf_op jit(solution)/shard_map/all_gather | solution.py:32
  318.6 10.4 %fusion.16 = f32[4096,256]{1,0:T(8,128)} fusion(bf16[2048,4096]{1,0:T(8,128)(2,1)} %all-gather.12.cloned.1.call-done, bf16[2048,256]{1,0:T(8,128)(2,1)S(1)} %copy-done.1), kind=kOutput, calls=%fused_computation.30 | convolution fusion | flops 4294967296 | bytes 22020096 | tf_op jit(solution)/shard_map/dot_general | solution.py:14
  329.1 0.5 all-gather.16.cloned.1.call-update
  329.7 0.1 compare_reduce_fusion
  329.8 0.4 copy-done.2
  330.2 1.3 multiply_convert_fusion
  331.6 0.2 reduce-scatter.6.cloned.1.call-start
  331.8 13.1 %convolution_convert_fusion = bf16[4096,256]{1,0:T(8,128)(2,1)} fusion(bf16[2048,4096]{1,0:T(8,128)(2,1)} %all-gather.12.cloned.1.call-done, bf16[2048,256]{1,0:T(8,128)(2,1)} %multiply_convert_fusion), kind=kOutput, calls=%fused_computation.5 | convolution fusion | flops 4296015872 | bytes 19922944 | tf_op jit(solution)/shard_map/dot_general | solution.py:14
  344.9 36.7 %reduce-scatter.4.cloned.1.call-done = f32[2048,256]{1,0:T(8,128)} async-done(((f32[4096,256]{1,0:T(8,128)}), f32[2048,256]{1,0:T(8,128)}) %reduce-scatter.4.cloned.1.call-update) | async-done | bytes 2097168 | tf_op jit(solution)/shard_map/reduce_scatter | solution.py:37
  381.6 2.9 subtract_convert_fusion.1
  384.5 0.3 all-gather.20.cloned.1.call-start
  384.8 31.4 %all-gather.16.cloned.1.call-done = bf16[4096,256]{1,0:T(8,128)(2,1)} async-done(((bf16[2048,256]{1,0:T(8,128)(2,1)}), bf16[4096,256]{1,0:T(8,128)(2,1)}) %all-gather.16.cloned.1.call-update) | async-done | bytes 2097168 | tf_op jit(solution)/shard_map/all_gather | solution.py:28
  416.3 12.5 %fusion.17 = f32[2048,256]{1,0:T(8,128)} fusion(bf16[2048,4096]{1,0:T(8,128)(2,1)} %all-gather.12.cloned.1.call-done, bf16[4096,256]{1,0:T(8,128)(2,1)} %all-gather.16.cloned.1.call-done), kind=kOutput, calls=%fused_computation.31 | convolution fusion | flops 4294967296 | bytes 20971520 | tf_op jit(solution)/shard_map/dot_general | solution.py:10
  428.7 22.7 %all-gather.18.cloned.1.call-done = bf16[4096,256]{1,0:T(8,128)(2,1)} async-done(((bf16[2048,256]{1,0:T(8,128)(2,1)}), bf16[4096,256]{1,0:T(8,128)(2,1)}) %all-gather.18.cloned.1.call-update) | async-done | bytes 2097168 | tf_op jit(solution)/shard_map/all_gather | solution.py:27
  451.5 11.8 %fusion.10 = bf16[2048,256]{1,0:T(8,128)(2,1)S(1)} fusion(f32[2048,256]{1,0:T(8,128)} %fusion.17, bf16[2048,4096]{1,0:T(8,128)(2,1)} %all-gather.8.cloned.1.call-done, bf16[4096,256]{1,0:T(8,128)(2,1)} %all-gather.18.cloned.1.call-done, f32[2048]{0:T(1024)S(1)} %convert_negate_fusion), kind=kOutput, calls=%fused_computation.11 | convolution fusion | flops 4296540160 | bytes 22028288 | tf_op jit(solution)/shard_map/dot_general | solution.py:10
  463.3 22.4 %reduce-scatter.6.cloned.1.call-done = bf16[2048,256]{1,0:T(8,128)(2,1)} async-done(((bf16[4096,256]{1,0:T(8,128)(2,1)}), bf16[2048,256]{1,0:T(8,128)(2,1)}) %reduce-scatter.6.cloned.1.call-update) | async-done | bytes 1048592 | tf_op jit(solution)/shard_map/reduce_scatter | solution.py:40
  485.7 133.1 %all-gather.14.cloned.1.call-done = bf16[2048,4096]{1,0:T(8,128)(2,1)} async-done(((bf16[2048,256]{1,0:T(8,128)(2,1)}), bf16[2048,4096]{1,0:T(8,128)(2,1)}) %all-gather.14.cloned.1.call-update) | async-done | bytes 16777232 | tf_op jit(solution)/shard_map/all_gather | solution.py:39
  618.8 8.7 fusion.12
  627.5 1.0 copy-done.7
  628.5 1.4 pad_maximum_fusion
  629.9 0.3 reduce-scatter.8.cloned.1.call-start
  630.2 175.0 %all-gather.20.cloned.1.call-done = bf16[4096,4096]{1,0:T(8,128)(2,1)} async-done(((bf16[4096,256]{1,0:T(8,128)(2,1)}), bf16[4096,4096]{1,0:T(8,128)(2,1)}) %all-gather.20.cloned.1.call-update) | async-done | bytes 33554448 | tf_op jit(solution)/shard_map/all_gather | solution.py:48
  805.2 8.4 fusion
  813.6 12.9 %fusion.4 = f32[4096,256]{1,0:T(8,128)} fusion(f32[4096,256]{1,0:T(8,128)S(1)} %fusion, bf16[2048,256]{1,0:T(8,128)(2,1)S(1)} %copy-done.3, bf16[4096,4096]{1,0:T(8,128)(2,1)} %all-gather.20.cloned.1.call-done), kind=kOutput, calls=%fused_computation.4 | convolution fusion | flops 4296015872 | bytes 26214400 | tf_op jit(solution)/shard_map/dot_general | solution.py:14
  826.5 53.3 %reduce-scatter.8.cloned.1.call-done = f32[2048,256]{1,0:T(8,128)} async-done(((f32[4096,256]{1,0:T(8,128)}), f32[2048,256]{1,0:T(8,128)}) %reduce-scatter.8.cloned.1.call-update) | async-done | bytes 2097168 | tf_op jit(solution)/shard_map/reduce_scatter | solution.py:52
  879.9 2.8 subtract_convert_fusion
  (34 shorter events, 0.4 us)
Async XLA Ops:
  7.2 38.2 %all-gather.10.cloned.1.call-start = ((), (), s32[]{:S(2)}) async-start(), calls=%async_computation.4 | async-start | bytes 3145728 | tf_op jit(solution)/shard_map/all_gather | solution.py:26
  7.9 170.0 %all-gather.8.cloned.1.call-start = ((), (), s32[]{:S(2)}) async-start(), calls=%async_computation.3 | async-start | bytes 17825792 | tf_op jit(solution)/shard_map/all_gather | solution.py:30
  8.6 310.0 %copy-start.1 = (bf16[2048,256]{1,0:T(8,128)(2,1)S(1)}, bf16[2048,256]{1,0:T(8,128)(2,1)}, u32[]{:S(2)}) copy-start(bf16[2048,256]{1,0:T(8,128)(2,1)} %param.8) | copy-start | bytes 3145732
  8.7 310.0 %all-gather.12.cloned.1.call-start = ((), (), s32[]{:S(2)}) async-start(), calls=%async_computation.5 | async-start | bytes 17825792 | tf_op jit(solution)/shard_map/all_gather | solution.py:32
  190.0 191.7 %reduce-scatter.4.cloned.1.call-start = ((), (), s32[]{:S(2)}) async-start(), calls=%async_computation.6 | async-start | bytes 6291456 | tf_op jit(solution)/shard_map/reduce_scatter | solution.py:37
  329.0 0.7 copy-start.8
  329.0 1.2 copy-start.2
  329.0 87.2 %all-gather.16.cloned.1.call-start = ((), (), s32[]{:S(2)}) async-start(), calls=%async_computation.8 | async-start | bytes 3145728 | tf_op jit(solution)/shard_map/all_gather | solution.py:28
  329.6 121.9 %all-gather.18.cloned.1.call-start = ((), (), s32[]{:S(2)}) async-start(), calls=%async_computation.10 | async-start | bytes 3145728 | tf_op jit(solution)/shard_map/all_gather | solution.py:27
  331.6 154.1 %reduce-scatter.6.cloned.1.call-start = ((), (), s32[]{:S(2)}) async-start(), calls=%async_computation.9 | async-start | bytes 3145728 | tf_op jit(solution)/shard_map/reduce_scatter | solution.py:40
  344.9 36.8 %copy-start.4 = (bf16[2048,256]{1,0:T(8,128)(2,1)S(1)}, bf16[2048,256]{1,0:T(8,128)(2,1)}, u32[]{:S(2)}) copy-start(bf16[2048,256]{1,0:T(8,128)(2,1)} %param.9) | copy-start | bytes 3145732
  344.9 273.9 %all-gather.14.cloned.1.call-start = ((), (), s32[]{:S(2)}) async-start(), calls=%async_computation.7 | async-start | bytes 17825792 | tf_op jit(solution)/shard_map/all_gather | solution.py:39
  384.5 420.7 %all-gather.20.cloned.1.call-start = ((), (), s32[]{:S(2)}) async-start(), calls=%async_computation.11 | async-start | bytes 35651584 | tf_op jit(solution)/shard_map/all_gather | solution.py:48
  428.7 190.1 %copy-start.9 = (bf16[4096,256]{1,0:T(8,128)(2,1)S(1)}, bf16[4096,256]{1,0:T(8,128)(2,1)}, u32[]{:S(2)}) copy-start(bf16[4096,256]{1,0:T(8,128)(2,1)} %all-gather.16.cloned.1.call-done) | copy-start | bytes 6291460
  463.3 164.2 %copy-start.6 = (bf16[2048,256]{1,0:T(8,128)(2,1)}, bf16[2048,256]{1,0:T(8,128)(2,1)S(1)}, u32[]{:S(2)}) copy-start(bf16[2048,256]{1,0:T(8,128)(2,1)S(1)} %fusion.10) | copy-start | bytes 3145732
  627.5 1.0 copy-start.7
  629.9 175.3 %copy-start = (bf16[2048,256]{1,0:T(8,128)(2,1)S(1)}, bf16[2048,256]{1,0:T(8,128)(2,1)}, u32[]{:S(2)}) copy-start(bf16[2048,256]{1,0:T(8,128)(2,1)} %multiply_convert_fusion) | copy-start | bytes 3145732
  629.9 183.7 %copy-start.3 = (bf16[2048,256]{1,0:T(8,128)(2,1)S(1)}, bf16[2048,256]{1,0:T(8,128)(2,1)}, u32[]{:S(2)}) copy-start(bf16[2048,256]{1,0:T(8,128)(2,1)} %param.10) | copy-start | bytes 3145732
  629.9 249.9 %reduce-scatter.8.cloned.1.call-start = ((), (), s32[]{:S(2)}) async-start(), calls=%async_computation.12 | async-start | bytes 6291456 | tf_op jit(solution)/shard_map/reduce_scatter | solution.py:52
  826.5 53.4 %copy-start.5 = (bf16[2048,256]{1,0:T(8,128)(2,1)S(1)}, bf16[2048,256]{1,0:T(8,128)(2,1)}, u32[]{:S(2)}) copy-start(bf16[2048,256]{1,0:T(8,128)(2,1)} %param.12) | copy-start | bytes 3145732
Sparse Core Ops, SparseCore 0:
  9.5 35.7 all-gather.9
  47.5 130.3 all-gather.7
  190.1 128.5 all-gather.11
  329.1 52.4 reduce-scatter.3
  383.1 33.1 all-gather.15
  418.3 33.1 all-gather.17
  453.8 31.8 reduce-scatter.5
  488.4 130.3 all-gather.13
  630.0 175.1 all-gather.19
  826.7 53.1 reduce-scatter.7
where the time goes:
time: 890 us; the launch traced here: 889 us
  waiting for transfers between devices  775 us (87%)
  matrix products  89.6 us (10%)
  between operations  14.3 us (2%)
    all_gather x1, waiting for transfers between devices, body(): block_part = lax.all_gather(stacked, 'col', axis=1, tiled=True)  175 us
    all_gather x1, waiting for transfers between devices, body(): lax.all_gather(top_diag, 'col', axis=1, tiled=True)  133 us
    all_gather x1, waiting for transfers between devices, body(): lax.all_gather(sigma_anc, 'col', axis=1, tiled=True)  133 us
    all_gather x1, waiting for transfers between devices, body(): block_part = lax.all_gather(top_off, 'col', axis=1, tiled=True)  129 us
    reduce_scatter x1, waiting for transfers between devices, body(): lax.psum_scatter(low_terms, 'row', scatter_dimension=0, tiled=True)  53.3 us
    dot_general x4, matrix products, times_rows(): return jnp.dot(block_part, columns, preferred_element_type=jnp.float32)  44.9 us
    dot_general x4, matrix products, inner_rows(): lax.dot_general(left, right, (((0,), (0,)), ((), ())), preferred_element_...  44.7 us
    reduce_scatter x1, waiting for transfers between devices, body(): lax.psum_scatter(terms[:, :width_here], 'row', scatter_dimension=0, tiled...  36.7 us
  transfers between devices with their start and end apart: 10, of which 10 were waited for; matrix products, arithmetic and copies ran while one was open for 5% of the time, Pallas kernels for 0%

commit v1 on v0

v1 whole, which is shorter than its diff:
```python
import jax
import jax.numpy as jnp
from jax import lax
from jax.sharding import PartitionSpec as P

BLOCK = 128
F32 = jnp.float32
BF16 = jnp.bfloat16


def solution(mesh):
    R, C = mesh.shape["row"], mesh.shape["col"]
    n = C // 2
    hb = n // R
    order = list(range(0, n, 2)) + list(range(n - 1, 0, -2))
    place = [order.index(c) for c in range(n)]

    def ring_perm(shift):
        return [
            (c * 2 + k, order[(place[c] + shift) % n] * 2 + k) for c in range(n) for k in range(2)
        ]

    ring_perms = {1: ring_perm(1), -1: ring_perm(-1)}
    core_perm = [(i, i ^ 1) for i in range(C)]

    def core_swap(x):
        return lax.ppermute(x, "col", core_perm)

    def row_swap(x):
        return lax.ppermute(x, "row", [(0, 1), (1, 0)])

    def body(sigma, top_panel, top_dinv, low_upper, low_ancestor, low_dinv, low_rows):
        rows, w = sigma.shape
        r = lax.axis_index("row")
        col = lax.axis_index("col")
        c, k = col // 2, col % 2
        pos = jnp.asarray(place, jnp.int32)[c]

        def origin(shift):
            return jnp.asarray(order, jnp.int32)[(pos - shift + n) % n]

        def slot(chip):
            if R == 2:
                return ((chip // hb) ^ r) * hb + chip % hb
            return chip

        def ring_steps(x, forward, back):
            chunks = [(0, x)]
            a = b = x
            for s in range(1, max(forward, back) + 1):
                if s <= forward:
                    a = lax.ppermute(a, "col", ring_perms[1])
                    chunks.append((s, a))
                if s <= back:
                    b = lax.ppermute(b, "col", ring_perms[-1])
                    chunks.append((-s, b))
            return chunks, (a, b)

        lanes = []

        def ring(x, wide):
            if lanes:
                x, _ = lax.optimization_barrier((x, lanes[-1]))
            long, short = n // 2, n - 1 - n // 2
            chunks, last = ring_steps(x, *((long, short) if wide else (short, long)))
            lanes.append(last)
            return chunks

        def from_core(mine, theirs):
            first = jnp.where(k == 0, mine, theirs)
            second = jnp.where(k == 0, theirs, mine)
            return jnp.stack([first, second], axis=1).reshape(rows, mine.shape[-1])

        def core_columns(x):
            return jnp.concatenate([x, core_swap(x)], axis=-1)

        def panel(x):
            x4 = x.reshape(hb, 2, w, w)
            keep = lax.dynamic_index_in_dim(x4, k, 1, keepdims=False)
            send = lax.dynamic_index_in_dim(x4, 1 - k, 1, keepdims=False)
            here = jnp.concatenate([keep, core_swap(send)], axis=-1)
            if R == 2:
                return jnp.concatenate([here, row_swap(here)], axis=0)
            return lax.all_gather(here, "row", axis=0, tiled=True)

        def times(chunks, right):
            total = 0.0
            for shift, chunk in chunks:
                block = lax.dynamic_index_in_dim(right, slot(origin(shift)), 0, keepdims=False)
                total = total + jnp.dot(chunk, block, preferred_element_type=F32)
            return total[:, :w] + core_swap(total[:, w:].astype(BF16)).astype(F32)

        def times_t(pairs):
            out = jnp.zeros((n, w, 2 * w), BF16)
            for i in range(n):
                part = 0.0
                for chunks, right in pairs:
                    shift, chunk = chunks[i]
                    part = part + lax.dot_general(
                        chunk, right, (((0,), (0,)), ((), ())), preferred_element_type=F32
                    )
                out = lax.dynamic_update_index_in_dim(
                    out, part.astype(BF16), slot(origin(shift)), 0
                )
            if R == 2:
                return out[:hb].astype(F32) + row_swap(out[hb:]).astype(F32)
            return lax.psum_scatter(out, "row", scatter_dimension=0, tiled=True).astype(F32)

        row_ids = (r * rows + jnp.arange(rows, dtype=jnp.int32)) // BLOCK
        in_pattern = jnp.any(row_ids[:, None] == low_rows[None, :], axis=1)[:, None]
        masked = jnp.where(in_pattern, low_ancestor, jnp.zeros_like(low_ancestor))

        share = low_rows.shape[0] // R
        blocks = lax.dynamic_slice_in_dim(low_rows, r * share, share)

        def pack(x):
            if R == 2:
                both = jnp.concatenate([x, row_swap(x)], axis=0)
                rank = lambda b: ((b // (rows // BLOCK)) ^ r) * (rows // BLOCK) + b % (rows // BLOCK)
            else:
                both = lax.all_gather(x, "row", axis=0, tiled=True)
                rank = lambda b: b
            return jnp.concatenate(
                [
                    lax.dynamic_slice_in_dim(both, rank(blocks[i]) * BLOCK, BLOCK, 0)
                    for i in range(share)
                ],
                axis=0,
            )

        top_ring = ring(top_panel, True)
        upper_panel = panel(low_upper)
        sigma_ring = ring(sigma, False)
        top_right = panel(top_panel)
        dinv_ring = ring(top_dinv, True)
        packed = pack(low_ancestor)
        packed_ring = ring(packed, False)
        upper_ring = ring(low_upper, True)

        v = (masked.astype(F32) - times(top_ring, upper_panel)).astype(BF16)
        top_off = (-times(sigma_ring, top_right)).astype(BF16)
        x = (-times(sigma_ring, panel(v))).astype(BF16)
        low_anc = jnp.where(in_pattern, x, jnp.zeros_like(x))
        x_packed = core_columns(pack(x))

        def own_columns(y):
            return from_core(y[..., :w], core_swap(y[..., w:]))

        top_diag = (
            top_dinv.astype(F32) - own_columns(times_t([(top_ring, core_columns(top_off))]))
        ).astype(BF16)
        by_shift = lambda chunks: sorted(chunks, key=lambda item: item[0] % n)
        top_s, dinv_s, upper_s, packed_s = map(
            by_shift, (top_ring, dinv_ring, upper_ring, packed_ring)
        )
        low_top_k = (
            -times_t([(dinv_s, core_columns(low_upper)), (top_s, core_columns(x))])
        ).astype(BF16)
        other = core_swap(low_top_k)
        low_top_both = from_core(
            low_top_k, jnp.concatenate([other[..., w:], other[..., :w]], axis=-1)
        )
        low_top = low_top_both[:, :w]
        low_diag = (
            low_dinv.astype(F32)
            - own_columns(times_t([(packed_s, x_packed), (upper_s, low_top_both)]))
        ).astype(BF16)
        return (top_off, top_diag, low_top, low_anc, low_diag)

    spec = P("row", "col")
    return jax.shard_map(
        body, mesh=mesh, in_specs=(spec,) * 6 + (P(),), out_specs=(spec,) * 5, check_vma=False
    )
```

time: 890 us -> 540 us (0.61); the launches traced: 889 us -> 530 us
  waiting for transfers between devices: 775 us -> 224 us
  starting transfers between devices: 1.06 us -> 49.9 us
  local copies, waits for them, and re-layouts: 1.43 us -> 49.3 us
  matrix products: 89.6 us -> 136 us
  between operations: 14.3 us -> 51.6 us
  other arithmetic: 8.53 us -> 19.5 us
    all_gather x7 -> x0, waiting for transfers between devices: 660 us -> none  [the longest x1 175 us: body(): block_part = lax.all_gather(stacked, 'col', axis=1, tiled=True)]
    ppermute x0 -> x56, waiting for transfers between devices: none -> 224 us  [the longest x18 109 us: ring_steps(): a = lax.ppermute(a, 'col', ring_perms[1])]
    reduce_scatter x3 -> x0, waiting for transfers between devices: 112 us -> none  [the longest x1 53.3 us: body(): lax.psum_scatter(low_terms, 'row', scatter_dimension=0, tiled=True)]
    ppermute x0 -> x56, starting transfers between devices: none -> 49.9 us  [the longest x18 29.1 us: ring_steps(): a = lax.ppermute(a, 'col', ring_perms[1])]
    dot_general x8 -> x64, matrix products: 89.6 us -> 136 us  [the longest x24 93.4 us: times(): total = total + jnp.dot(chunk, block, preferred_element_type=F32)]
    unnamed x20 -> x78, local copies, waits for them, and re-layouts: 1.43 us -> 25.4 us
    slice x0 -> x11, local copies, waits for them, and re-layouts: none -> 10.5 us  [the longest x3 6.25 us: times(): return total[:, :w] + core_swap(total[:, w:].astype(BF16)).astype(F32)]
  transfers between devices with their start and end apart: 10 -> 56, of which waited for: 10 -> 23; matrix products, arithmetic and copies ran while one was open for 5% -> 37% of each run, Pallas kernels for 0% -> 0%
where the time goes in v1:
time: 540 us; the launch traced here: 530 us
  waiting for transfers between devices  224 us (41%)
  matrix products  136 us (25%)
  between operations  51.6 us (10%)
  starting transfers between devices  49.9 us (9%)
  local copies, waits for them, and re-layouts  49.3 us (9%)
  other arithmetic  19.5 us (4%)
    ppermute x18, waiting for transfers between devices, ring_steps(): a = lax.ppermute(a, 'col', ring_perms[1])  109 us
    dot_general x24, matrix products, times(): total = total + jnp.dot(chunk, block, preferred_element_type=F32)  93.4 us
    ppermute x17, waiting for transfers between devices, ring_steps(): b = lax.ppermute(b, 'col', ring_perms[-1])  86.8 us
    dot_general x40, matrix products, times_t(): lax.dot_general(chunk, right, (((0,), (0,)), ((), ())), preferred_element...  42.5 us
    ppermute x18, starting transfers between devices, ring_steps(): a = lax.ppermute(a, 'col', ring_perms[1])  29.1 us
    ppermute x8, waiting for transfers between devices, row_swap(): return lax.ppermute(x, 'row', [(0, 1), (1, 0)])  28.2 us
    unnamed x78, local copies, waits for them, and re-layouts  25.4 us
  transfers between devices with their start and end apart: 56, of which 23 were waited for; matrix products, arithmetic and copies ran while one was open for 37% of the time, Pallas kernels for 0%

profile of v1, /device:TPU:0, one launch (start us, length us, event | category | flops | bytes accessed | tf_op | source)
XLA Modules:
  0.0 530.1 jit_solution(7129256301175794697)
XLA Ops:
  18.5 10.5 %collective-permute-done = bf16[2048,256]{1,0:T(8,128)(2,1)} collective-permute-done((bf16[2048,256]{1,0:T(8,128)(2,1)S(1)}, bf16[2048,256]{1,0:T(8,128)(2,1)}, u32[]{:S(2)}, u32[]{:S(2)}) %collective-permute-start) | collective-permute-done | bytes 1048608 | tf_op jit(solution)/shard_map/ppermute | solution.py:52
  91.0 15.8 %collective-permute-done.5 = bf16[2048,256]{1,0:T(8,128)(2,1)S(1)} collective-permute-done((bf16[2048,256]{1,0:T(8,128)(2,1)}, bf16[2048,256]{1,0:T(8,128)(2,1)S(1)}, u32[]{:S(2)}, u32[]{:S(2)}) %collective-permute-start.5) | collective-permute-done | bytes 1048608 | tf_op jit(solution)/shard_map/ppermute | solution.py:55
  110.9 4.0 fusion.94
  117.7 12.3 %collective-permute-done.6 = bf16[2048,256]{1,0:T(8,128)(2,1)S(1)} collective-permute-done((bf16[2048,256]{1,0:T(8,128)(2,1)S(1)}, bf16[2048,256]{1,0:T(8,128)(2,1)S(1)}, u32[]{:S(2)}, u32[]{:S(2)}) %collective-permute-start.6) | collective-permute-done | bytes 1048608 | tf_op jit(solution)/shard_map/ppermute | solution.py:55
  132.8 9.5 %add_bitcast_fusion = f32[2048,512]{0,1:T(8,128)} fusion(f32[512,2048]{1,0:T(8,128)} %fusion.88, f32[512,2048]{1,0:T(8,128)} %fusion.90, f32[512,2048]{1,0:T(8,128)S(1)} %fusion.92, f32[512,2048]{1,0:T(8,128)} %fusion.94, f32[512,2048]{1,0:T(8,128)S(1)} %fusion.96, f32[512,2048]{1,0:T(8,128)S(1)} %fusion.100, f32[512,2048]{1,0:T(8,128)S(1)} %fusion.98, ...), kind=kOutput, calls=%fused_computation | convolution fusion | flops 544210944 | bytes 34865156 | tf_op jit(solution)/shard_map/dot_general | solution.py:90
  159.7 3.5 constant_dynamic-slice_fusion.1
  163.2 3.5 copy.116
  166.7 8.4 %collective-permute-done.10 = bf16[2048,256]{1,0:T(8,128)(2,1)} collective-permute-done((bf16[2048,256]{1,0:T(8,128)(2,1)}, bf16[2048,256]{1,0:T(8,128)(2,1)}, u32[]{:S(2)}, u32[]{:S(2)}) %collective-permute-start.10) | collective-permute-done | bytes 1048608 | tf_op jit(solution)/shard_map/ppermute | solution.py:55
  177.1 4.0 fusion.115
  189.0 11.1 %collective-permute-done.12 = bf16[2048,256]{1,0:T(8,128)(2,1)} collective-permute-done((bf16[2048,256]{1,0:T(8,128)(2,1)}, bf16[2048,256]{1,0:T(8,128)(2,1)}, u32[]{:S(2)}, u32[]{:S(2)}) %collective-permute-start.12) | collective-permute-done | bytes 1048608 | tf_op jit(solution)/shard_map/ppermute | solution.py:55
  204.1 4.0 fusion.109
  209.9 4.7 fusion.85
  214.6 4.0 fusion.77
  218.6 4.0 fusion.79
  222.6 4.1 fusion.81
  226.7 4.0 fusion.83
  243.1 11.2 %collective-permute-done.15 = bf16[2048,256]{1,0:T(8,128)(2,1)S(1)} collective-permute-done((bf16[2048,256]{1,0:T(8,128)(2,1)S(1)}, bf16[2048,256]{1,0:T(8,128)(2,1)S(1)}, u32[]{:S(2)}, u32[]{:S(2)}) %collective-permute-start.15) | collective-permute-done | bytes 1048608 | tf_op jit(solution)/shard_map/ppermute | solution.py:55
  256.4 13.6 %add_add_fusion = f32[2048,512]{0,1:T(8,128)} fusion(f32[2048,512]{0,1:T(8,128)} %fusion.73, f32[2048,512]{0,1:T(8,128)} %fusion.75, f32[2048,512]{0,1:T(8,128)} %fusion.77, f32[2048,512]{0,1:T(8,128)} %fusion.79, f32[2048,512]{0,1:T(8,128)} %fusion.81, f32[2048,512]{0,1:T(8,128)} %fusion.85, f32[2048,512]{0,1:T(8,128)} %fusion.83, ...), kind=kOutput, calls=%fused_computation.1 | convolution fusion | flops 544210944 | bytes 34865156 | tf_op jit(solution)/shard_map/dot_general | solution.py:90
  272.7 9.4 %add_add_fusion.1 = f32[2048,512]{0,1:T(8,128)} fusion(f32[2048,512]{0,1:T(8,128)} %fusion.103, f32[2048,512]{0,1:T(8,128)} %fusion.105, f32[2048,512]{0,1:T(8,128)S(1)} %fusion.107, f32[2048,512]{0,1:T(8,128)} %fusion.109, f32[2048,512]{0,1:T(8,128)S(1)} %fusion.111, f32[2048,512]{0,1:T(8,128)S(1)} %copy-done, f32[2048,512]{0,1:T(8,128)S(1)} %fusion.113, ...), kind=kOutput, calls=%fused_computation.2 | convolution fusion | flops 544210944 | bytes 34865156 | tf_op jit(solution)/shard_map/dot_general | solution.py:90
  295.1 17.0 %collective-permute-done.38 = bf16[2048,256]{0,1:T(8,128)(2,1)S(1)} collective-permute-done((bf16[2048,256]{0,1:T(8,128)(2,1)S(1)}, bf16[2048,256]{0,1:T(8,128)(2,1)S(1)}, u32[]{:S(2)}, u32[]{:S(2)}) %collective-permute-start.38) | collective-permute-done | bytes 1048608 | tf_op jit(solution)/shard_map/ppermute | solution.py:30
  312.7 5.5 %collective-permute-done.29 = bf16[2048,256]{1,0:T(8,128)(2,1)S(1)} collective-permute-done((bf16[2048,256]{1,0:T(8,128)(2,1)}, bf16[2048,256]{1,0:T(8,128)(2,1)S(1)}, u32[]{:S(2)}, u32[]{:S(2)}) %collective-permute-start.29) | collective-permute-done | bytes 1048608 | tf_op jit(solution)/shard_map/ppermute | solution.py:52
  333.3 9.6 %collective-permute-done.30 = bf16[2048,256]{1,0:T(8,128)(2,1)S(1)} collective-permute-done((bf16[2048,256]{1,0:T(8,128)(2,1)S(1)}, bf16[2048,256]{1,0:T(8,128)(2,1)S(1)}, u32[]{:S(2)}, u32[]{:S(2)}) %collective-permute-start.30) | collective-permute-done | bytes 1048608 | tf_op jit(solution)/shard_map/ppermute | solution.py:52
  350.0 16.8 %collective-permute-done.31 = bf16[2048,256]{1,0:T(8,128)(2,1)S(1)} collective-permute-done((bf16[2048,256]{1,0:T(8,128)(2,1)S(1)}, bf16[2048,256]{1,0:T(8,128)(2,1)S(1)}, u32[]{:S(2)}, u32[]{:S(2)}) %collective-permute-start.31) | collective-permute-done | bytes 1048608 | tf_op jit(solution)/shard_map/ppermute | solution.py:52
  373.6 6.8 %collective-permute-done.43 = bf16[1024,256]{1,0:T(8,128)(2,1)S(1)} collective-permute-done((bf16[1024,256]{1,0:T(8,128)(2,1)S(1)}, bf16[1024,256]{1,0:T(8,128)(2,1)S(1)}, u32[]{:S(2)}, u32[]{:S(2)}) %collective-permute-start.43) | collective-permute-done | bytes 524320 | tf_op jit(solution)/shard_map/ppermute | solution.py:55
  386.5 6.0 %collective-permute-done.44 = bf16[1024,256]{1,0:T(8,128)(2,1)S(1)} collective-permute-done((bf16[1024,256]{1,0:T(8,128)(2,1)S(1)}, bf16[1024,256]{1,0:T(8,128)(2,1)S(1)}, u32[]{:S(2)}, u32[]{:S(2)}) %collective-permute-start.44) | collective-permute-done | bytes 524320 | tf_op jit(solution)/shard_map/ppermute | solution.py:55
  398.0 6.4 %collective-permute-done.45 = bf16[1024,256]{1,0:T(8,128)(2,1)S(1)} collective-permute-done((bf16[1024,256]{1,0:T(8,128)(2,1)S(1)}, bf16[1024,256]{1,0:T(8,128)(2,1)S(1)}, u32[]{:S(2)}, u32[]{:S(2)}) %collective-permute-start.45) | collective-permute-done | bytes 524320 | tf_op jit(solution)/shard_map/ppermute | solution.py:55
  406.3 8.8 %collective-permute-done.46 = bf16[1024,256]{1,0:T(8,128)(2,1)S(1)} collective-permute-done((bf16[1024,256]{1,0:T(8,128)(2,1)S(1)}, bf16[1024,256]{1,0:T(8,128)(2,1)S(1)}, u32[]{:S(2)}, u32[]{:S(2)}) %collective-permute-start.46) | collective-permute-done | bytes 524320 | tf_op jit(solution)/shard_map/ppermute | solution.py:55
  421.1 17.4 %collective-permute-done.47 = bf16[2048,256]{1,0:T(8,128)(2,1)S(1)} collective-permute-done((bf16[2048,256]{1,0:T(8,128)(2,1)}, bf16[2048,256]{1,0:T(8,128)(2,1)S(1)}, u32[]{:S(2)}, u32[]{:S(2)}) %collective-permute-start.47) | collective-permute-done | bytes 1048608 | tf_op jit(solution)/shard_map/ppermute | solution.py:52
  444.3 17.6 %collective-permute-done.48 = bf16[2048,256]{1,0:T(8,128)(2,1)S(1)} collective-permute-done((bf16[2048,256]{1,0:T(8,128)(2,1)S(1)}, bf16[2048,256]{1,0:T(8,128)(2,1)S(1)}, u32[]{:S(2)}, u32[]{:S(2)}) %collective-permute-start.48) | collective-permute-done | bytes 1048608 | tf_op jit(solution)/shard_map/ppermute | solution.py:52
  466.6 18.3 %collective-permute-done.49 = bf16[2048,256]{1,0:T(8,128)(2,1)S(1)} collective-permute-done((bf16[2048,256]{1,0:T(8,128)(2,1)S(1)}, bf16[2048,256]{1,0:T(8,128)(2,1)S(1)}, u32[]{:S(2)}, u32[]{:S(2)}) %collective-permute-start.49) | collective-permute-done | bytes 1048608 | tf_op jit(solution)/shard_map/ppermute | solution.py:52
  489.2 11.1 %collective-permute-done.50 = bf16[2048,256]{1,0:T(8,128)(2,1)S(1)} collective-permute-done((bf16[2048,256]{1,0:T(8,128)(2,1)S(1)}, bf16[2048,256]{1,0:T(8,128)(2,1)S(1)}, u32[]{:S(2)}, u32[]{:S(2)}) %collective-permute-start.50) | collective-permute-done | bytes 1048608 | tf_op jit(solution)/shard_map/ppermute | solution.py:52
  509.7 9.6 %collective-permute-done.54 = bf16[4,256,512]{2,1,0:T(8,128)(2,1)} collective-permute-done((bf16[4,256,512]{2,1,0:T(8,128)(2,1)}, bf16[4,256,512]{2,1,0:T(8,128)(2,1)}, u32[]{:S(2)}, u32[]{:S(2)}) %collective-permute-start.54) | collective-permute-done | bytes 1048608 | tf_op jit(solution)/shard_map/ppermute | solution.py:30
  (278 shorter events, 186.1 us)
Async XLA Ops:
  2.6 26.5 %collective-permute-start = (bf16[2048,256]{1,0:T(8,128)(2,1)S(1)}, bf16[2048,256]{1,0:T(8,128)(2,1)}, u32[]{:S(2)}, u32[]{:S(2)}) collective-permute-start(bf16[2048,256]{1,0:T(8,128)(2,1)S(1)} %copy-done.12), channel_id=1, source_target_pairs={{0,4},{1,5},{2,0},{3,1},{4,8},{5,9},{6,2},{7,3},{8,12},{9,13},{10,... | collective-permute-start | bytes 3145736 | tf_op jit(solution)/shard_map/ppermute | solution.py:52
  5.2 77.0 %collective-permute-start.4 = (bf16[2048,256]{1,0:T(8,128)(2,1)S(1)}, bf16[2048,256]{1,0:T(8,128)(2,1)}, u32[]{:S(2)}, u32[]{:S(2)}) collective-permute-start(bf16[2048,256]{1,0:T(8,128)(2,1)S(1)} %copy-done.12), channel_id=1, source_target_pairs={{0,2},{1,3},{2,6},{3,7},{4,0},{5,1},{6,10},{7,11},{8,4},{9,5},{10,... | collective-permute-start | bytes 3145736 | tf_op jit(solution)/shard_map/ppermute | solution.py:55
  6.4 76.4 %collective-permute-start.22 = (bf16[4,256,512]{2,1,0:T(8,128)(2,1)}, bf16[4,256,512]{2,1,0:T(8,128)(2,1)}, u32[]{:S(2)}, u32[]{:S(2)}) collective-permute-start(bf16[4,256,512]{2,1,0:T(8,128)(2,1)} %pad_maximum_fusion.9), channel_id=1, source_target_pairs={{0,16},{16,0},{1,17},{17,1},{2,18},{18,2},{3,19},{19,3},{4,20},{20... | collective-permute-start | bytes 3145736 | tf_op jit(solution)/shard_map/ppermute | solution.py:30
  8.3 282.8 %collective-permute-start.20 = (bf16[2048,256]{1,0:T(8,128)(2,1)}, bf16[2048,256]{1,0:T(8,128)(2,1)}, u32[]{:S(2)}, u32[]{:S(2)}) collective-permute-start(bf16[2048,256]{1,0:T(8,128)(2,1)} %param.59), channel_id=1, source_target_pairs={{0,1},{1,0},{2,3},{3,2},{4,5},{5,4},{6,7},{7,6},{8,9},{9,8},{10,11... | collective-permute-start | bytes 3145736 | tf_op jit(solution)/shard_map/ppermute | solution.py:27
  8.4 71.2 %collective-permute-start.7 = (bf16[4,256,256]{2,1,0:T(8,128)(2,1)S(1)}, bf16[4,256,256]{2,1,0:T(8,128)(2,1)S(1)}, u32[]{:S(2)}, u32[]{:S(2)}) collective-permute-start(bf16[4,256,256]{2,1,0:T(8,128)(2,1)S(1)} %get-tuple-element.43), channel_id=1, source_target_pairs={{0,1},{1,0},{2,3},{3,2},{4,5},{5,4},{6,7},{7,6},{8,9},{9,8},{10,11... | collective-permute-start | bytes 1572872 | tf_op jit(solution)/shard_map/ppermute | solution.py:27
  29.0 56.2 %collective-permute-start.1 = (bf16[2048,256]{1,0:T(8,128)(2,1)}, bf16[2048,256]{1,0:T(8,128)(2,1)}, u32[]{:S(2)}, u32[]{:S(2)}) collective-permute-start(bf16[2048,256]{1,0:T(8,128)(2,1)} %collective-permute-done), channel_id=1, source_target_pairs={{0,4},{1,5},{2,0},{3,1},{4,8},{5,9},{6,2},{7,3},{8,12},{9,13},{10,... | collective-permute-start | bytes 3145736 | tf_op jit(solution)/shard_map/ppermute | solution.py:52
  79.6 64.6 %collective-permute-start.37 = (bf16[2048,256]{1,0:T(8,128)(2,1)}, bf16[2048,256]{1,0:T(8,128)(2,1)}, u32[]{:S(2)}, u32[]{:S(2)}) collective-permute-start(bf16[2048,256]{1,0:T(8,128)(2,1)} %param.60), channel_id=1, source_target_pairs={{0,16},{16,0},{1,17},{17,1},{2,18},{18,2},{3,19},{19,3},{4,20},{20... | collective-permute-start | bytes 3145736 | tf_op jit(solution)/shard_map/ppermute | solution.py:30
  82.2 71.7 %collective-permute-start.8 = (bf16[4,256,512]{2,1,0:T(8,128)(2,1)}, bf16[4,256,512]{2,1,0:T(8,128)(2,1)}, u32[]{:S(2)}, u32[]{:S(2)}) collective-permute-start(bf16[4,256,512]{2,1,0:T(8,128)(2,1)} %pad_maximum_fusion.8), channel_id=1, source_target_pairs={{0,16},{16,0},{1,17},{17,1},{2,18},{18,2},{3,19},{19,3},{4,20},{20... | collective-permute-start | bytes 3145736 | tf_op jit(solution)/shard_map/ppermute | solution.py:30
  82.7 24.1 %collective-permute-start.5 = (bf16[2048,256]{1,0:T(8,128)(2,1)}, bf16[2048,256]{1,0:T(8,128)(2,1)S(1)}, u32[]{:S(2)}, u32[]{:S(2)}) collective-permute-start(bf16[2048,256]{1,0:T(8,128)(2,1)} %collective-permute-done.4), channel_id=1, source_target_pairs={{0,2},{1,3},{2,6},{3,7},{4,0},{5,1},{6,10},{7,11},{8,4},{9,5},{10,... | collective-permute-start | bytes 3145736 | tf_op jit(solution)/shard_map/ppermute | solution.py:55
  85.2 24.1 %collective-permute-start.2 = (bf16[2048,256]{1,0:T(8,128)(2,1)}, bf16[2048,256]{1,0:T(8,128)(2,1)S(1)}, u32[]{:S(2)}, u32[]{:S(2)}) collective-permute-start(bf16[2048,256]{1,0:T(8,128)(2,1)} %collective-permute-done.1), channel_id=1, source_target_pairs={{0,4},{1,5},{2,0},{3,1},{4,8},{5,9},{6,2},{7,3},{8,12},{9,13},{10,... | collective-permute-start | bytes 3145736 | tf_op jit(solution)/shard_map/ppermute | solution.py:52
  149.2 25.9 %collective-permute-start.10 = (bf16[2048,256]{1,0:T(8,128)(2,1)}, bf16[2048,256]{1,0:T(8,128)(2,1)}, u32[]{:S(2)}, u32[]{:S(2)}) collective-permute-start(bf16[2048,256]{1,0:T(8,128)(2,1)} %param.56), channel_id=1, source_target_pairs={{0,2},{1,3},{2,6},{3,7},{4,0},{5,1},{6,10},{7,11},{8,4},{9,5},{10,... | collective-permute-start | bytes 3145736 | tf_op jit(solution)/shard_map/ppermute | solution.py:55
  150.1 25.9 %collective-permute-start.9 = (bf16[2048,256]{1,0:T(8,128)(2,1)}, bf16[2048,256]{1,0:T(8,128)(2,1)}, u32[]{:S(2)}, u32[]{:S(2)}) collective-permute-start(bf16[2048,256]{1,0:T(8,128)(2,1)} %param.56), channel_id=1, source_target_pairs={{0,4},{1,5},{2,0},{3,1},{4,8},{5,9},{6,2},{7,3},{8,12},{9,13},{10,... | collective-permute-start | bytes 3145736 | tf_op jit(solution)/shard_map/ppermute | solution.py:52
  175.0 25.1 %collective-permute-start.12 = (bf16[2048,256]{1,0:T(8,128)(2,1)}, bf16[2048,256]{1,0:T(8,128)(2,1)}, u32[]{:S(2)}, u32[]{:S(2)}) collective-permute-start(bf16[2048,256]{1,0:T(8,128)(2,1)} %collective-permute-done.10), channel_id=1, source_target_pairs={{0,2},{1,3},{2,6},{3,7},{4,0},{5,1},{6,10},{7,11},{8,4},{9,5},{10,... | collective-permute-start | bytes 3145736 | tf_op jit(solution)/shard_map/ppermute | solution.py:55
  176.0 25.1 %collective-permute-start.11 = (bf16[2048,256]{1,0:T(8,128)(2,1)}, bf16[2048,256]{1,0:T(8,128)(2,1)}, u32[]{:S(2)}, u32[]{:S(2)}) collective-permute-start(bf16[2048,256]{1,0:T(8,128)(2,1)} %collective-permute-done.9), channel_id=1, source_target_pairs={{0,4},{1,5},{2,0},{3,1},{4,8},{5,9},{6,2},{7,3},{8,12},{9,13},{10,... | collective-permute-start | bytes 3145736 | tf_op jit(solution)/shard_map/ppermute | solution.py:52
  185.5 24.3 %collective-permute-start.25 = (bf16[4,256,512]{2,1,0:T(8,128)(2,1)S(1)}, bf16[4,256,512]{2,1,0:T(8,128)(2,1)S(1)}, u32[]{:S(2)}, u32[]{:S(2)}) collective-permute-start(bf16[4,256,512]{2,1,0:T(8,128)(2,1)S(1)} %pad_maximum_fusion.10), channel_id=1, source_target_pairs={{0,16},{16,0},{1,17},{17,1},{2,18},{18,2},{3,19},{19,3},{4,20},{20... | collective-permute-start | bytes 3145736 | tf_op jit(solution)/shard_map/ppermute | solution.py:30
  200.1 30.5 %collective-permute-start.14 = (bf16[2048,256]{1,0:T(8,128)(2,1)}, bf16[2048,256]{1,0:T(8,128)(2,1)S(1)}, u32[]{:S(2)}, u32[]{:S(2)}) collective-permute-start(bf16[2048,256]{1,0:T(8,128)(2,1)} %collective-permute-done.12), channel_id=1, source_target_pairs={{0,2},{1,3},{2,6},{3,7},{4,0},{5,1},{6,10},{7,11},{8,4},{9,5},{10,... | collective-permute-start | bytes 3145736 | tf_op jit(solution)/shard_map/ppermute | solution.py:55
  201.1 36.6 %collective-permute-start.13 = (bf16[2048,256]{1,0:T(8,128)(2,1)}, bf16[2048,256]{1,0:T(8,128)(2,1)S(1)}, u32[]{:S(2)}, u32[]{:S(2)}) collective-permute-start(bf16[2048,256]{1,0:T(8,128)(2,1)} %collective-permute-done.11), channel_id=1, source_target_pairs={{0,4},{1,5},{2,0},{3,1},{4,8},{5,9},{6,2},{7,3},{8,12},{9,13},{10,... | collective-permute-start | bytes 3145736 | tf_op jit(solution)/shard_map/ppermute | solution.py:52
  254.3 38.2 %collective-permute-start.28 = (bf16[2048,256]{1,0:T(8,128)(2,1)}, bf16[2048,256]{1,0:T(8,128)(2,1)}, u32[]{:S(2)}, u32[]{:S(2)}) collective-permute-start(bf16[2048,256]{1,0:T(8,128)(2,1)} %param.58), channel_id=1, source_target_pairs={{0,4},{1,5},{2,0},{3,1},{4,8},{5,9},{6,2},{7,3},{8,12},{9,13},{10,... | collective-permute-start | bytes 3145736 | tf_op jit(solution)/shard_map/ppermute | solution.py:52
  255.9 38.7 %collective-permute-start.32 = (bf16[2048,256]{1,0:T(8,128)(2,1)}, bf16[2048,256]{1,0:T(8,128)(2,1)}, u32[]{:S(2)}, u32[]{:S(2)}) collective-permute-start(bf16[2048,256]{1,0:T(8,128)(2,1)} %param.58), channel_id=1, source_target_pairs={{0,2},{1,3},{2,6},{3,7},{4,0},{5,1},{6,10},{7,11},{8,4},{9,5},{10,... | collective-permute-start | bytes 3145736 | tf_op jit(solution)/shard_map/ppermute | solution.py:55
  287.0 25.1 %collective-permute-start.38 = (bf16[2048,256]{0,1:T(8,128)(2,1)S(1)}, bf16[2048,256]{0,1:T(8,128)(2,1)S(1)}, u32[]{:S(2)}, u32[]{:S(2)}) collective-permute-start(bf16[2048,256]{0,1:T(8,128)(2,1)S(1)} %get-tuple-element.29), channel_id=1, source_target_pairs={{0,16},{16,0},{1,17},{17,1},{2,18},{18,2},{3,19},{19,3},{4,20},{20... | collective-permute-start | bytes 3145736 | tf_op jit(solution)/shard_map/ppermute | solution.py:30
  292.4 27.4 %collective-permute-start.27 = (bf16[2048,256]{0,1:T(8,128)(2,1)S(1)}, bf16[2048,256]{0,1:T(8,128)(2,1)S(1)}, u32[]{:S(2)}, u32[]{:S(2)}) collective-permute-start(bf16[2048,256]{0,1:T(8,128)(2,1)S(1)} %get-tuple-element.29), channel_id=1, source_target_pairs={{0,1},{1,0},{2,3},{3,2},{4,5},{5,4},{6,7},{7,6},{8,9},{9,8},{10,11... | collective-permute-start | bytes 3145736 | tf_op jit(solution)/shard_map/ppermute | solution.py:27
  292.5 25.8 %collective-permute-start.29 = (bf16[2048,256]{1,0:T(8,128)(2,1)}, bf16[2048,256]{1,0:T(8,128)(2,1)S(1)}, u32[]{:S(2)}, u32[]{:S(2)}) collective-permute-start(bf16[2048,256]{1,0:T(8,128)(2,1)} %collective-permute-done.28), channel_id=1, source_target_pairs={{0,4},{1,5},{2,0},{3,1},{4,8},{5,9},{6,2},{7,3},{8,12},{9,13},{10,... | collective-permute-start | bytes 3145736 | tf_op jit(solution)/shard_map/ppermute | solution.py:52
  294.4 35.8 %collective-permute-start.17 = (bf16[2048,256]{0,1:T(8,128)(2,1)S(1)}, bf16[2048,256]{0,1:T(8,128)(2,1)S(1)}, u32[]{:S(2)}, u32[]{:S(2)}) collective-permute-start(bf16[2048,256]{0,1:T(8,128)(2,1)S(1)} %fusion.5), channel_id=1, source_target_pairs={{0,1},{1,0},{2,3},{3,2},{4,5},{5,4},{6,7},{7,6},{8,9},{9,8},{10,11... | collective-permute-start | bytes 3145736 | tf_op jit(solution)/shard_map/ppermute | solution.py:27
  294.7 30.0 %collective-permute-start.33 = (bf16[2048,256]{1,0:T(8,128)(2,1)}, bf16[2048,256]{1,0:T(8,128)(2,1)S(1)}, u32[]{:S(2)}, u32[]{:S(2)}) collective-permute-start(bf16[2048,256]{1,0:T(8,128)(2,1)} %collective-permute-done.32), channel_id=1, source_target_pairs={{0,2},{1,3},{2,6},{3,7},{4,0},{5,1},{6,10},{7,11},{8,4},{9,5},{10,... | collective-permute-start | bytes 3145736 | tf_op jit(solution)/shard_map/ppermute | solution.py:55
  312.6 107.9 %collective-permute-start.39 = (bf16[1024,256]{0,1:T(8,128)(2,1)S(1)}, bf16[1024,256]{0,1:T(8,128)(2,1)S(1)}, u32[]{:S(2)}, u32[]{:S(2)}) collective-permute-start(bf16[1024,256]{0,1:T(8,128)(2,1)S(1)} %fusion.142), channel_id=1, source_target_pairs={{0,1},{1,0},{2,3},{3,2},{4,5},{5,4},{6,7},{7,6},{8,9},{9,8},{10,11... | collective-permute-start | bytes 1572872 | tf_op jit(solution)/shard_map/ppermute | solution.py:27
  318.2 24.7 %collective-permute-start.30 = (bf16[2048,256]{1,0:T(8,128)(2,1)S(1)}, bf16[2048,256]{1,0:T(8,128)(2,1)S(1)}, u32[]{:S(2)}, u32[]{:S(2)}) collective-permute-start(bf16[2048,256]{1,0:T(8,128)(2,1)S(1)} %collective-permute-done.29), channel_id=1, source_target_pairs={{0,4},{1,5},{2,0},{3,1},{4,8},{5,9},{6,2},{7,3},{8,12},{9,13},{10,... | collective-permute-start | bytes 3145736 | tf_op jit(solution)/shard_map/ppermute | solution.py:52
  324.7 25.3 %collective-permute-start.34 = (bf16[2048,256]{1,0:T(8,128)(2,1)S(1)}, bf16[2048,256]{1,0:T(8,128)(2,1)S(1)}, u32[]{:S(2)}, u32[]{:S(2)}) collective-permute-start(bf16[2048,256]{1,0:T(8,128)(2,1)S(1)} %collective-permute-done.33), channel_id=1, source_target_pairs={{0,2},{1,3},{2,6},{3,7},{4,0},{5,1},{6,10},{7,11},{8,4},{9,5},{10,... | collective-permute-start | bytes 3145736 | tf_op jit(solution)/shard_map/ppermute | solution.py:55
  343.0 23.8 %collective-permute-start.31 = (bf16[2048,256]{1,0:T(8,128)(2,1)S(1)}, bf16[2048,256]{1,0:T(8,128)(2,1)S(1)}, u32[]{:S(2)}, u32[]{:S(2)}) collective-permute-start(bf16[2048,256]{1,0:T(8,128)(2,1)S(1)} %collective-permute-done.30), channel_id=1, source_target_pairs={{0,4},{1,5},{2,0},{3,1},{4,8},{5,9},{6,2},{7,3},{8,12},{9,13},{10,... | collective-permute-start | bytes 3145736 | tf_op jit(solution)/shard_map/ppermute | solution.py:52
  373.0 32.0 %collective-permute-start.35 = (bf16[4,256,512]{2,1,0:T(8,128)(2,1)S(1)}, bf16[4,256,512]{2,1,0:T(8,128)(2,1)S(1)}, u32[]{:S(2)}, u32[]{:S(2)}) collective-permute-start(bf16[4,256,512]{2,1,0:T(8,128)(2,1)S(1)} %slice.130), channel_id=1, source_target_pairs={{0,16},{16,0},{1,17},{17,1},{2,18},{18,2},{3,19},{19,3},{4,20},{20... | collective-permute-start | bytes 3145736 | tf_op jit(solution)/shard_map/ppermute | solution.py:30
  419.9 84.8 %collective-permute-start.18 = (bf16[4,256,512]{2,1,0:T(8,128)(2,1)S(1)}, bf16[4,256,512]{2,1,0:T(8,128)(2,1)S(1)}, u32[]{:S(2)}, u32[]{:S(2)}) collective-permute-start(bf16[4,256,512]{2,1,0:T(8,128)(2,1)S(1)} %slice.122), channel_id=1, source_target_pairs={{0,16},{16,0},{1,17},{17,1},{2,18},{18,2},{3,19},{19,3},{4,20},{20... | collective-permute-start | bytes 3145736 | tf_op jit(solution)/shard_map/ppermute | solution.py:30
  441.0 23.7 %collective-permute-start.52 = (bf16[2048,256]{1,0:T(8,128)(2,1)S(1)}, bf16[2048,256]{1,0:T(8,128)(2,1)S(1)}, u32[]{:S(2)}, u32[]{:S(2)}) collective-permute-start(bf16[2048,256]{1,0:T(8,128)(2,1)S(1)} %collective-permute-done.51), channel_id=1, source_target_pairs={{0,2},{1,3},{2,6},{3,7},{4,0},{5,1},{6,10},{7,11},{8,4},{9,5},{10,... | collective-permute-start | bytes 3145736 | tf_op jit(solution)/shard_map/ppermute | solution.py:55
  464.7 23.8 %collective-permute-start.53 = (bf16[2048,256]{1,0:T(8,128)(2,1)S(1)}, bf16[2048,256]{1,0:T(8,128)(2,1)S(1)}, u32[]{:S(2)}, u32[]{:S(2)}) collective-permute-start(bf16[2048,256]{1,0:T(8,128)(2,1)S(1)} %collective-permute-done.52), channel_id=1, source_target_pairs={{0,2},{1,3},{2,6},{3,7},{4,0},{5,1},{6,10},{7,11},{8,4},{9,5},{10,... | collective-permute-start | bytes 3145736 | tf_op jit(solution)/shard_map/ppermute | solution.py:55
  (56 other events, 815.6 us)
